TPU v7x, 32 devices: a whole 2x2x4 slice. The times are simulated.
32 devices in a mesh: row: 2 (over core), lat: 8 (over z, x), grp: 2 (over y).
Axes of the slice: x: 2, y: 2, z: 4, core: 2. Of those that a mesh axis runs over, the one named last changes fastest.
Arguments:
- stream_in: bfloat16 [192, 3584], P(('lat', 'grp'), 'row'), may hold values from -36 to 36, as said below
- pre_gain: float32 [3584], P('row'), may hold values from 0.25 to 1.75
- gate_weight: bfloat16 [3584, 14336], P('row', ('lat', 'grp')), may hold values from -0.09375 to 0.09375
- up_weight: bfloat16 [3584, 14336], P('row', ('lat', 'grp')), may hold values from -0.09375 to 0.09375
- down_weight: bfloat16 [14336, 3584], P(('lat', 'grp'), 'row'), may hold values from -0.046875 to 0.046875
- post_gain: float32 [3584], P('row'), may hold values from 0.25 to 1.75
- enc_weight: float32 [3584, 16384], P('row', ('lat', 'grp')), may hold values from -0.09375 to 0.09375
- enc_bias: float32 [16384], P(('lat', 'grp')), may hold values from -3 to 3
- dec_weight: float32 [16384, 3584], P(('lat', 'grp'), 'row'), may hold values from -0.046875 to 0.046875
- dec_bias: float32 [3584], P('row'), may hold values from -3 to 3
Outputs:
- stream_out: bfloat16 [192, 3584], P(('lat', 'grp'), 'row')
- grad_enc: float32 [3584, 16384], P('row', ('lat', 'grp'))
- grad_enc_bias: float32 [16384], P(('lat', 'grp'))
- grad_dec: float32 [16384, 3584], P(('lat', 'grp'), 'row')
- grad_dec_bias: float32 [3584], P('row')
Inputs may be any that keep to these rules, and one draw needn't show every extreme that they name: `stream_in`: Real-valued activations with scales that differ over rows and features.
All inputs are finite; a program needn't handle non-finite values.
Results may differ from a plain program's by a relative error of at most 0.013.
Values may be sent and summed in bfloat16 or wider, within the bound.
A program may use at most 128 MiB of HBM per device.

v0:
```python
import math
import jax
import jax.numpy as jnp
from jax import lax
from jax.sharding import PartitionSpec as P

D = 3584
epsilon = 1e-06
sparsity = 0.2
sharpness = 4.0


def smooth_relu(value):
    return jax.nn.softplus(sharpness * value) / sharpness


def activate(summed, hidden_width):
    return (
        jax.nn.gelu(summed[:, :hidden_width], approximate=True) * summed[:, hidden_width:]
    ).astype(jnp.bfloat16)


def body(
    stream_in,
    pre_gain,
    gate_weight,
    up_weight,
    down_weight,
    post_gain,
    enc_weight,
    enc_bias,
    dec_weight,
    dec_bias,
):
    highest = lax.Precision.HIGHEST
    stream = stream_in.astype(jnp.float32)
    hidden_width = gate_weight.shape[1]
    squares = lax.psum(jnp.sum(stream * stream, axis=1), "row")
    normed = (stream * lax.rsqrt(squares[:, None] / D + epsilon) * pre_gain).astype(jnp.bfloat16)
    joined = jnp.concatenate([gate_weight, up_weight], axis=1)
    partial_proj = jnp.dot(
        lax.all_gather(normed, ("lat", "grp"), axis=0, tiled=True),
        joined,
        preferred_element_type=jnp.float32,
    )
    shares = lax.psum_scatter(partial_proj, "row", scatter_dimension=0, tiled=True)
    hidden = lax.all_gather(activate(shares, hidden_width), "row", axis=0, tiled=True)
    output = lax.psum_scatter(
        jnp.dot(hidden, down_weight, preferred_element_type=jnp.float32),
        ("lat", "grp"),
        scatter_dimension=0,
        tiled=True,
    )
    out_squares = lax.psum(jnp.sum(output * output, axis=1), "row")
    stream_out = (
        stream + output * lax.rsqrt(out_squares[:, None] / D + epsilon) * post_gain
    ).astype(jnp.bfloat16)
    relayed = lax.all_gather(stream_out, ("lat", "grp"), axis=0, tiled=True)
    inputs = relayed.astype(jnp.float32)
    scale = 1.0 / math.sqrt(inputs.shape[0])
    encoded = jnp.dot(inputs, enc_weight, precision=highest, preferred_element_type=jnp.float32)
    preact = lax.psum(encoded, "row") + enc_bias
    latents = smooth_relu(preact)
    partial_rec = jnp.dot(
        latents, dec_weight, precision=highest, preferred_element_type=jnp.float32
    )
    recon = lax.psum(partial_rec, ("lat", "grp"))
    residual_grad = (recon + dec_bias - inputs) * scale
    grad_dec = jnp.dot(
        latents.T, residual_grad, precision=highest, preferred_element_type=jnp.float32
    )
    grad_dec_bias = jnp.sum(residual_grad, axis=0)
    back_term = jnp.dot(
        residual_grad, dec_weight.T, precision=highest, preferred_element_type=jnp.float32
    )
    latent_grad = (
        lax.psum(back_term.astype(jnp.bfloat16), "row").astype(jnp.float32) + sparsity * scale
    )
    preact_grad = latent_grad * jax.nn.sigmoid(sharpness * preact)
    grad_enc = jnp.dot(inputs.T, preact_grad, precision=highest, preferred_element_type=jnp.float32)
    grad_enc_bias = jnp.sum(preact_grad, axis=0)
    return (stream_out, grad_enc, grad_enc_bias, grad_dec, grad_dec_bias)


def solution(mesh):
    placed = (
        P(("lat", "grp"), "row"),
        P("row"),
        P("row", ("lat", "grp")),
        P("row", ("lat", "grp")),
        P(("lat", "grp"), "row"),
        P("row"),
        P("row", ("lat", "grp")),
        P(("lat", "grp")),
        P(("lat", "grp"), "row"),
        P("row"),
    )
    return jax.shard_map(
        body,
        mesh=mesh,
        in_specs=placed,
        out_specs=(
            P(("lat", "grp"), "row"),
            P("row", ("lat", "grp")),
            P(("lat", "grp")),
            P(("lat", "grp"), "row"),
            P("row"),
        ),
        check_vma=False,
    )
```

profile of v0, /device:TPU:0, one launch (start us, length us, event | category | flops | bytes accessed | tf_op | source)
XLA Modules:
  0.0 402.0 jit_solution(2031803251081122726)
XLA Ops:
  7.2 0.0 copy-start
  7.2 0.0 reduce-scatter.4.cloned.1.call-start
  7.2 1.1 fusion.20
  8.3 2.6 psum.35
  10.9 0.9 fusion.24
  11.8 50.0 %all-gather = bf16[16,12,1792]{2,1,0:T(8,128)(2,1)} all-gather(bf16[1,12,1792]{2,1,0:T(8,128)(2,1)S(1)} %fusion.24), channel_id=1, replica_groups=mesh['row'=2,'lat'=8,'grp'=2] {'lat','grp'}, dimensions={0}, use_global_device_ids=true | all-gather | bytes 731136 | tf_op jit(solution)/shard_map/all_gather | solution.py:42
  61.9 2.1 reshape.23
  63.9 5.6 %fusion.1 = f32[192,1792]{1,0:T(8,128)} fusion(bf16[192,1792]{1,0:T(8,128)(2,1)} %reshape.23, bf16[1792,896]{1,0:T(8,128)(2,1)} %param.13, bf16[1792,896]{1,0:T(8,128)(2,1)} %param.12), kind=kOutput, calls=%fused_computation | convolution fusion | flops 1245970432 | bytes 8486912 | tf_op jit(solution)/shard_map/dot_general | solution.py:41
  69.5 0.0 reduce-scatter.4.cloned.1.call-update
  69.6 0.0 all-reduce.6.cloned.1.call-start
  69.6 4.8 %reduce-scatter.4.cloned.1.call-done = f32[96,1792]{1,0:T(8,128)} async-done(((f32[192,1792]{1,0:T(8,128)}), f32[96,1792]{1,0:T(8,128)}) %reduce-scatter.4.cloned.1.call-update) | async-done | bytes 688144 | tf_op jit(solution)/shard_map/reduce_scatter | solution.py:46
  74.4 1.2 fusion.14
  75.6 2.1 all_gather.10
  77.7 0.0 copy-done
  77.7 0.0 copy-start.9
  77.7 2.0 fusion.36
  79.6 0.0 copy-start.4
  79.6 0.0 copy-start.8
  79.6 52.9 %fusion = f32[16,1792]{1,0:T(8,128)S(1)} fusion(f32[192,1792]{1,0:T(8,128)} %fusion.36), kind=kCustom, calls=%all-reduce-scatter | all-reduce-scatter fusion | flops 458753 | bytes 1491456
  132.6 1.3 collective-permute-start.2
  133.9 4.5 %collective-permute-start.1 = (f32[16,1792]{1,0:T(8,128)S(1)}, f32[16,1792]{1,0:T(8,128)}, u32[]{:S(2)}, u32[]{:S(2)}) collective-permute-start(f32[16,1792]{1,0:T(8,128)S(1)} %fusion), channel_id=1, source_target_pairs={{0,2},{1,3},{2,4},{3,5},{4,6},{5,7},{6,8},{7,9},{8,10},{9,11},{10,... | collective-permute-start | bytes 344072
  138.4 2.2 collective-permute-start
  140.5 0.7 slice.10
  141.2 2.4 collective-permute-start.3
  143.6 0.0 copy-done.9
  143.6 0.6 dynamic-slice.4
  144.8 0.8 collective-permute-done.3
  145.6 0.0 collective-permute-done.2
  145.6 0.0 collective-permute-done.1
  145.6 0.0 collective-permute-done
  145.6 8.0 %concatenate.4 = f32[76,1792]{1,0:T(8,128)} concatenate(f32[12,1792]{1,0:T(8,128)} %collective-permute-done.3, f32[16,1792]{1,0:T(8,128)S(1)} %collective-permute-done.2, f32[16,1792]{1,0:T(8,128)} %collective-permute-done.1, f32[16,1792]{1,0:T(8,128)} %collective-permute-done, f32[16,1792]{1,0:T(8,128)S(1)} %fusion), dimensions={0} | concatenate | bytes 1089536
  153.6 1.0 multiply_reduce_fusion
  154.6 2.5 psum.36
  157.1 0.0 copy-done.4
  157.1 0.0 copy-done.8
  157.1 1.0 fusion.23
  158.1 0.0 copy-start.5
  158.2 47.7 %all-gather.1 = bf16[16,12,1792]{2,1,0:T(8,128)(2,1)} all-gather(bf16[1,12,1792]{2,1,0:T(8,128)(2,1)S(1)} %bitcast.14), channel_id=1, replica_groups=mesh['row'=2,'lat'=8,'grp'=2] {'lat','grp'}, dimensions={0}, use_global_device_ids=true | all-gather | bytes 731136 | tf_op jit(solution)/shard_map/all_gather | solution.py:58
  205.8 2.1 reshape.25
  207.9 0.0 copy-start.6
  207.9 7.3 %fusion.37 = f32[192,1024]{1,0:T(8,128)} fusion(bf16[192,1792]{1,0:T(8,128)(2,1)} %reshape.25, f32[1792,1024]{1,0:T(8,128)} %param.16), kind=kOutput, calls=%fused_computation.46 | convolution fusion | flops 4227858432 | bytes 8814592 | tf_op jit(solution)/shard_map/dot_general | solution.py:61
  215.2 0.0 copy-done.5
  215.2 0.0 all-reduce.6.cloned.1.call-update
  215.3 0.0 copy-start.7
  215.3 0.2 all-reduce.8.cloned.1.call-start
  215.5 15.0 %all-reduce.6.cloned.1.call-done = f32[192,1024]{1,0:T(8,128)} async-done(((f32[192,1024]{1,0:T(8,128)}), f32[192,1024]{1,0:T(8,128)}) %all-reduce.6.cloned.1.call-update) | async-done | bytes 786448 | tf_op jit(solution)/shard_map/psum | solution.py:62
  230.5 0.0 copy-done.6
  230.5 9.9 %fusion.17 = f32[192,1792]{1,0:T(8,128)} fusion(f32[1024,1792]{1,0:T(8,128)} %param.18, f32[192,1024]{1,0:T(8,128)} %all-reduce.6.cloned.1.call-done, f32[1024]{0:T(1024)S(1)} %copy-done.6), kind=kOutput, calls=%fused_computation.21 | convolution fusion | flops 4229627904 | bytes 9506816 | tf_op jit(solution)/shard_map/dot_general | solution.py:64
  240.4 0.0 all-reduce.8.cloned.1.call-update
  240.4 0.3 all-reduce.10.cloned.1.call-start
  240.7 116.4 %all-reduce.8.cloned.1.call-done = f32[192,1792]{1,0:T(8,128)} async-done(((f32[192,1792]{1,0:T(8,128)}), f32[192,1792]{1,0:T(8,128)}) %all-reduce.8.cloned.1.call-update) | async-done | bytes 1376272 | tf_op jit(solution)/shard_map/psum | solution.py:67
  357.0 0.0 copy-done.7
  357.0 12.0 %convolution_convert_fusion = bf16[192,1024]{1,0:T(8,128)(2,1)} fusion(f32[1024,1792]{1,0:T(8,128)} %param.18, bf16[192,1792]{1,0:T(8,128)(2,1)} %reshape.25, f32[192,1792]{1,0:T(8,128)} %all-reduce.8.cloned.1.call-done, f32[1792]{0:T(1024)S(1)} %copy-done.7), kind=kOutput, calls=%fused_computation.6 | convolution fusion | flops 4229431296 | bytes 9804800 | tf_op jit(solution)/shard_map/dot_general | solution.py:73
  369.0 0.0 all-reduce.10.cloned.1.call-update
  369.0 0.0 copy-start.1
  369.0 0.0 copy-start.3
  369.0 2.5 fusion.19
  371.5 0.0 copy-done.1
  371.5 0.0 copy-done.3
  371.5 10.1 %fusion.15 = f32[1024,1792]{1,0:T(8,128)} fusion(f32[192,1024]{1,0:T(8,128)S(1)} %copy-done.3, f32[1024]{0:T(1024)S(1)} %copy-done.6, bf16[192,1792]{1,0:T(8,128)(2,1)S(1)} %copy-done.1, f32[192,1792]{1,0:T(8,128)} %all-reduce.8.cloned.1.call-done, f32[1792]{0:T(1024)S(1)} %copy-done.7), kind=kOutput, calls=%fused_computation.20 | convolution fusion | flops 4231004160 | bytes 10202112 | tf_op jit(solution)/shard_map/dot_general | solution.py:69
  381.6 5.0 %all-reduce.10.cloned.1.call-done = bf16[192,1024]{1,0:T(8,128)(2,1)} async-done(((bf16[192,1024]{1,0:T(8,128)(2,1)}), bf16[192,1024]{1,0:T(8,128)(2,1)}) %all-reduce.10.cloned.1.call-update) | async-done | bytes 393232 | tf_op jit(solution)/shard_map/psum | solution.py:77
  386.6 2.2 fusion.34
  388.8 0.0 copy-done.2
  388.8 6.7 %fusion.35 = f32[1792,1024]{1,0:T(8,128)} fusion(bf16[192,1792]{1,0:T(8,128)(2,1)S(1)} %copy-done.2, bf16[192,1024]{1,0:T(8,128)(2,1)} %all-reduce.10.cloned.1.call-done, f32[192,1024]{1,0:T(8,128)} %all-reduce.6.cloned.1.call-done, f32[1024]{0:T(1024)S(1)} %copy-done.6), kind=kOutput, calls=%fused_computation.44 | convolution fusion | flops 4229431296 | bytes 9211904 | tf_op jit(solution)/shard_map/dot_general | solution.py:80
  (3 shorter events, 0.0 us)
Async XLA Ops:
  7.2 70.5 %copy-start = (bf16[896,1792]{1,0:T(8,128)(2,1)S(1)}, bf16[896,1792]{1,0:T(8,128)(2,1)}, u32[]{:S(2)}) copy-start(bf16[896,1792]{1,0:T(8,128)(2,1)} %param.14) | copy-start | bytes 9633796
  7.2 67.2 %reduce-scatter.4.cloned.1.call-start = ((), (), s32[]{:S(2)}) async-start(), calls=%async_computation.1 | async-start | bytes 2064384 | tf_op jit(solution)/shard_map/reduce_scatter | solution.py:46
  69.6 160.9 %all-reduce.6.cloned.1.call-start = ((), (), s32[]{:S(2)}) async-start(), calls=%async_computation.2 | async-start | bytes 1572864 | tf_op jit(solution)/shard_map/psum | solution.py:62
  77.7 65.9 %copy-start.9 = (u32[32]{0:T(128)S(1)}, u32[32]{0:T(128)}, u32[]{:S(2)}) copy-start(u32[32]{0:T(128)} %constant.30) | copy-start | bytes 388
  79.6 77.5 %copy-start.4 = (bf16[12,1792]{1,0:T(8,128)(2,1)S(1)}, bf16[12,1792]{1,0:T(8,128)(2,1)}, u32[]{:S(2)}) copy-start(bf16[12,1792]{1,0:T(8,128)(2,1)} %param.10) | copy-start | bytes 129028
  79.6 77.5 %copy-start.8 = (f32[1792]{0:T(1024)S(1)}, f32[1792]{0:T(1024)}, u32[]{:S(2)}) copy-start(f32[1792]{0:T(1024)} %param.15) | copy-start | bytes 21508
  132.6 13.1 %collective-permute-start.2 = (f32[16,1792]{1,0:T(8,128)S(1)}, f32[16,1792]{1,0:T(8,128)S(1)}, u32[]{:S(2)}, u32[]{:S(2)}) collective-permute-start(f32[16,1792]{1,0:T(8,128)S(1)} %fusion), channel_id=1, source_target_pairs={{0,3},{1,4},{2,5},{3,6},{4,7},{5,8},{6,9},{7,10},{8,11},{9,12},{10... | collective-permute-start | bytes 344072
  133.9 11.8 %collective-permute-start.1 = (f32[16,1792]{1,0:T(8,128)S(1)}, f32[16,1792]{1,0:T(8,128)}, u32[]{:S(2)}, u32[]{:S(2)}) collective-permute-start(f32[16,1792]{1,0:T(8,128)S(1)} %fusion), channel_id=1, source_target_pairs={{0,2},{1,3},{2,4},{3,5},{4,6},{5,7},{6,8},{7,9},{8,10},{9,11},{10,... | collective-permute-start | bytes 344072
  138.4 7.3 %collective-permute-start = (f32[16,1792]{1,0:T(8,128)S(1)}, f32[16,1792]{1,0:T(8,128)}, u32[]{:S(2)}, u32[]{:S(2)}) collective-permute-start(f32[16,1792]{1,0:T(8,128)S(1)} %fusion), channel_id=1, source_target_pairs={{0,1},{1,2},{2,3},{3,4},{4,5},{5,6},{6,7},{7,8},{8,9},{9,10},{10,1... | collective-permute-start | bytes 344072
  141.2 4.4 %collective-permute-start.3 = (f32[12,1792]{1,0:T(8,128)}, f32[12,1792]{1,0:T(8,128)}, u32[]{:S(2)}, u32[]{:S(2)}) collective-permute-start(f32[12,1792]{1,0:T(8,128)} %slice.10), channel_id=1, source_target_pairs={{0,4},{1,5},{2,6},{3,7},{4,8},{5,9},{6,10},{7,11},{8,12},{9,13},{1... | collective-permute-start | bytes 258056
  158.1 57.1 %copy-start.5 = (bf16[12,1792]{1,0:T(8,128)(2,1)}, bf16[12,1792]{1,0:T(8,128)(2,1)S(1)}, u32[]{:S(2)}) copy-start(bf16[12,1792]{1,0:T(8,128)(2,1)S(1)} %fusion.23) | copy-start | bytes 129028
  207.9 22.6 %copy-start.6 = (f32[1024]{0:T(1024)S(1)}, f32[1024]{0:T(1024)}, u32[]{:S(2)}) copy-start(f32[1024]{0:T(1024)} %param.17) | copy-start | bytes 12292
  215.3 141.7 %copy-start.7 = (f32[1792]{0:T(1024)S(1)}, f32[1792]{0:T(1024)}, u32[]{:S(2)}) copy-start(f32[1792]{0:T(1024)} %param.19) | copy-start | bytes 21508
  215.3 141.7 %all-reduce.8.cloned.1.call-start = ((), (), s32[]{:S(2)}) async-start(), calls=%async_computation.3 | async-start | bytes 2752512 | tf_op jit(solution)/shard_map/psum | solution.py:67
  240.4 146.2 %all-reduce.10.cloned.1.call-start = ((), (), s32[]{:S(2)}) async-start(), calls=%async_computation.4 | async-start | bytes 786432 | tf_op jit(solution)/shard_map/psum | solution.py:77
  369.0 2.5 copy-start.1
  369.0 2.5 copy-start.3
  386.6 2.2 copy-start.2
Sparse Core Ops, SparseCore 0:
  69.7 4.6 reduce-scatter.3
  215.4 15.0 all-reduce.5
  240.5 116.4 all-reduce.7
  369.1 17.4 all-reduce.9
where the time goes:
time: 403 us; the launch traced here: 402 us
  blocking collectives  158 us (39%)
  waiting for transfers between devices  142 us (35%)
  matrix products  53.5 us (13%)
  between operations  14.5 us (4%)
  local copies, waits for them, and re-layouts  13.4 us (3%)
  starting transfers between devices  10.9 us (3%)
  other arithmetic  9.95 us (2%)
    psum x1, waiting for transfers between devices, body(): recon = lax.psum(partial_rec, ('lat', 'grp'))  116 us
    unnamed x1, blocking collectives  52.9 us
    all_gather x1, blocking collectives, body(): lax.all_gather(normed, ('lat', 'grp'), axis=0, tiled=True)  50 us
    all_gather x1, blocking collectives, body(): relayed = lax.all_gather(stream_out, ('lat', 'grp'), axis=0, tiled=True)  47.7 us
    psum x1, waiting for transfers between devices, body(): preact = lax.psum(encoded, 'row') + enc_bias  15 us
    unnamed x25, local copies, waits for them, and re-layouts  13.4 us
    dot_general x1, matrix products, body(): jnp.dot(residual_grad, dec_weight.T, precision=highest, preferred_element...  12 us
    unnamed x4, starting transfers between devices  10.4 us
  transfers between devices with their start and end apart: 8, of which 5 were waited for; matrix products, arithmetic and copies ran while one was open for 3% of the time, Pallas kernels for 0%

commit v1 on v0

--- a/solution.py
+++ b/solution.py
@@ -64,7 +64,8 @@
     partial_rec = jnp.dot(
         latents, dec_weight, precision=highest, preferred_element_type=jnp.float32
     )
-    recon = lax.psum(partial_rec, ("lat", "grp"))
+    partial = lax.psum(partial_rec, "grp")
+    recon = lax.psum(partial, "lat")
     residual_grad = (recon + dec_bias - inputs) * scale
     grad_dec = jnp.dot(
         latents.T, residual_grad, precision=highest, preferred_element_type=jnp.float32

time: 403 us -> 423 us (1.050)
  waiting for transfers between devices: 142 us -> 162 us
    psum x1 -> x2, waiting for transfers between devices: 116 us -> 136 us  [the longest x1 87.9 us: body(): recon = lax.psum(partial, 'lat')]
  transfers between devices with their start and end apart: 8 -> 9, of which waited for: 5 -> 6; matrix products, arithmetic and copies ran while one was open for 3% -> 3% of each run, Pallas kernels for 0% -> 0%
where the time goes in v1:
time: 423 us; the launch traced here: 422 us
  waiting for transfers between devices  162 us (38%)
  blocking collectives  158 us (37%)
  matrix products  53.5 us (13%)
  between operations  14.5 us (3%)
  local copies, waits for them, and re-layouts  13.4 us (3%)
  starting transfers between devices  11 us (3%)
  other arithmetic  9.95 us (2%)
    psum x1, waiting for transfers between devices, body(): recon = lax.psum(partial, 'lat')  87.9 us
    unnamed x1, blocking collectives  52.9 us
    all_gather x1, blocking collectives, body(): lax.all_gather(normed, ('lat', 'grp'), axis=0, tiled=True)  50 us
    psum x1, waiting for transfers between devices, body(): partial = lax.psum(partial_rec, 'grp')  48.5 us
    all_gather x1, blocking collectives, body(): relayed = lax.all_gather(stream_out, ('lat', 'grp'), axis=0, tiled=True)  47.7 us
    psum x1, waiting for transfers between devices, body(): preact = lax.psum(encoded, 'row') + enc_bias  15 us
    unnamed x25, local copies, waits for them, and re-layouts  13.4 us
    dot_general x1, matrix products, body(): jnp.dot(residual_grad, dec_weight.T, precision=highest, preferred_element...  12 us
  transfers between devices with their start and end apart: 9, of which 6 were waited for; matrix products, arithmetic and copies ran while one was open for 3% of the time, Pallas kernels for 0%

profile of v1, /device:TPU:0, one launch (start us, length us, event | category | flops | bytes accessed | tf_op | source)
XLA Modules:
  0.0 422.4 jit_solution(6897547855615704474)
XLA Ops:
  7.2 0.0 copy-start
  7.2 0.0 reduce-scatter.4.cloned.1.call-start
  7.2 1.1 fusion.20
  8.3 2.6 psum.42
  10.9 0.9 fusion.24
  11.8 50.0 %all-gather = bf16[16,12,1792]{2,1,0:T(8,128)(2,1)} all-gather(bf16[1,12,1792]{2,1,0:T(8,128)(2,1)S(1)} %fusion.24), channel_id=1, replica_groups=mesh['row'=2,'lat'=8,'grp'=2] {'lat','grp'}, dimensions={0}, use_global_device_ids=true | all-gather | bytes 731136 | tf_op jit(solution)/shard_map/all_gather | solution.py:42
  61.9 2.1 reshape.23
  63.9 5.6 %fusion.1 = f32[192,1792]{1,0:T(8,128)} fusion(bf16[192,1792]{1,0:T(8,128)(2,1)} %reshape.23, bf16[1792,896]{1,0:T(8,128)(2,1)} %param.13, bf16[1792,896]{1,0:T(8,128)(2,1)} %param.12), kind=kOutput, calls=%fused_computation | convolution fusion | flops 1245970432 | bytes 8486912 | tf_op jit(solution)/shard_map/dot_general | solution.py:41
  69.5 0.0 reduce-scatter.4.cloned.1.call-update
  69.6 0.0 all-reduce.7.cloned.1.call-start
  69.6 4.8 %reduce-scatter.4.cloned.1.call-done = f32[96,1792]{1,0:T(8,128)} async-done(((f32[192,1792]{1,0:T(8,128)}), f32[96,1792]{1,0:T(8,128)}) %reduce-scatter.4.cloned.1.call-update) | async-done | bytes 688144 | tf_op jit(solution)/shard_map/reduce_scatter | solution.py:46
  74.4 1.2 fusion.14
  75.6 2.1 all_gather.10
  77.7 0.0 copy-done
  77.7 0.0 copy-start.9
  77.7 2.0 fusion.36
  79.6 0.0 copy-start.4
  79.6 52.9 %fusion = f32[16,1792]{1,0:T(8,128)S(1)} fusion(f32[192,1792]{1,0:T(8,128)} %fusion.36), kind=kCustom, calls=%all-reduce-scatter | all-reduce-scatter fusion | flops 458753 | bytes 1491456
  132.6 1.3 collective-permute-start.2
  133.9 4.5 %collective-permute-start.1 = (f32[16,1792]{1,0:T(8,128)S(1)}, f32[16,1792]{1,0:T(8,128)}, u32[]{:S(2)}, u32[]{:S(2)}) collective-permute-start(f32[16,1792]{1,0:T(8,128)S(1)} %fusion), channel_id=1, source_target_pairs={{0,2},{1,3},{2,4},{3,5},{4,6},{5,7},{6,8},{7,9},{8,10},{9,11},{10,... | collective-permute-start | bytes 344072
  138.4 2.2 collective-permute-start
  140.5 0.7 slice.10
  141.2 2.4 collective-permute-start.3
  143.6 0.0 copy-done.9
  143.6 0.6 dynamic-slice.4
  144.8 0.8 collective-permute-done.3
  145.6 0.0 collective-permute-done.2
  145.6 0.0 collective-permute-done.1
  145.6 0.0 collective-permute-done
  145.6 8.0 %concatenate.4 = f32[76,1792]{1,0:T(8,128)} concatenate(f32[12,1792]{1,0:T(8,128)} %collective-permute-done.3, f32[16,1792]{1,0:T(8,128)S(1)} %collective-permute-done.2, f32[16,1792]{1,0:T(8,128)} %collective-permute-done.1, f32[16,1792]{1,0:T(8,128)} %collective-permute-done, f32[16,1792]{1,0:T(8,128)S(1)} %fusion), dimensions={0} | concatenate | bytes 1089536
  153.6 1.0 multiply_reduce_fusion
  154.6 2.5 psum.43
  157.1 0.0 copy-done.4
  157.1 0.0 copy-done.8
  157.1 1.0 fusion.23
  158.1 0.0 copy-start.5
  158.2 47.7 %all-gather.1 = bf16[16,12,1792]{2,1,0:T(8,128)(2,1)} all-gather(bf16[1,12,1792]{2,1,0:T(8,128)(2,1)S(1)} %bitcast.14), channel_id=1, replica_groups=mesh['row'=2,'lat'=8,'grp'=2] {'lat','grp'}, dimensions={0}, use_global_device_ids=true | all-gather | bytes 731136 | tf_op jit(solution)/shard_map/all_gather | solution.py:58
  205.8 2.1 reshape.25
  207.9 7.3 %fusion.37 = f32[192,1024]{1,0:T(8,128)} fusion(bf16[192,1792]{1,0:T(8,128)(2,1)} %reshape.25, f32[1792,1024]{1,0:T(8,128)} %param.16), kind=kOutput, calls=%fused_computation.46 | convolution fusion | flops 4227858432 | bytes 8814592 | tf_op jit(solution)/shard_map/dot_general | solution.py:61
  215.2 0.0 copy-done.5
  215.2 0.0 all-reduce.7.cloned.1.call-update
  215.3 0.2 all-reduce.9.cloned.1.call-start
  215.5 15.0 %all-reduce.7.cloned.1.call-done = f32[192,1024]{1,0:T(8,128)} async-done(((f32[192,1024]{1,0:T(8,128)}), f32[192,1024]{1,0:T(8,128)}) %all-reduce.7.cloned.1.call-update) | async-done | bytes 786448 | tf_op jit(solution)/shard_map/psum | solution.py:62
  230.5 0.0 copy-done.6
  230.5 9.9 %fusion.17 = f32[192,1792]{1,0:T(8,128)} fusion(f32[1024,1792]{1,0:T(8,128)} %param.18, f32[192,1024]{1,0:T(8,128)} %all-reduce.7.cloned.1.call-done, f32[1024]{0:T(1024)S(1)} %copy-done.6), kind=kOutput, calls=%fused_computation.21 | convolution fusion | flops 4229627904 | bytes 9506816 | tf_op jit(solution)/shard_map/dot_general | solution.py:64
  240.4 0.0 all-reduce.9.cloned.1.call-update
  240.4 0.0 all-reduce.11.cloned.1.call-start
  240.4 48.5 %all-reduce.9.cloned.1.call-done = f32[192,1792]{1,0:T(8,128)} async-done(((f32[192,1792]{1,0:T(8,128)}), f32[192,1792]{1,0:T(8,128)}) %all-reduce.9.cloned.1.call-update) | async-done | bytes 1376272 | tf_op jit(solution)/shard_map/psum | solution.py:67
  288.9 0.0 all-reduce.11.cloned.1.call-update
  288.9 0.3 all-reduce.13.cloned.1.call-start
  289.2 87.9 %all-reduce.11.cloned.1.call-done = f32[192,1792]{1,0:T(8,128)} async-done(((f32[192,1792]{1,0:T(8,128)}), f32[192,1792]{1,0:T(8,128)}) %all-reduce.11.cloned.1.call-update) | async-done | bytes 1376272 | tf_op jit(solution)/shard_map/psum | solution.py:68
  377.1 0.0 copy-done.7
  377.1 12.0 %convolution_convert_fusion = bf16[192,1024]{1,0:T(8,128)(2,1)} fusion(f32[1024,1792]{1,0:T(8,128)} %param.18, bf16[192,1792]{1,0:T(8,128)(2,1)} %reshape.25, f32[192,1792]{1,0:T(8,128)} %all-reduce.11.cloned.1.call-done, f32[1792]{0:T(1024)S(1)} %copy-done.7), kind=kOutput, calls=%fused_computation.6 | convolution fusion | flops 4229431296 | bytes 9804800 | tf_op jit(solution)/shard_map/dot_general | solution.py:74
  389.1 0.0 all-reduce.13.cloned.1.call-update
  389.1 0.0 copy-start.1
  389.2 0.0 copy-start.3
  389.2 2.5 fusion.19
  391.7 0.0 copy-done.1
  391.7 0.0 copy-done.3
  391.7 10.1 %fusion.15 = f32[1024,1792]{1,0:T(8,128)} fusion(f32[192,1024]{1,0:T(8,128)S(1)} %copy-done.3, f32[1024]{0:T(1024)S(1)} %copy-done.6, bf16[192,1792]{1,0:T(8,128)(2,1)S(1)} %copy-done.1, f32[192,1792]{1,0:T(8,128)} %all-reduce.11.cloned.1.call-done, f32[1792]{0:T(1024)S(1)} %copy-done.7), kind=kOutput, calls=%fused_computation.20 | convolution fusion | flops 4231004160 | bytes 10202112 | tf_op jit(solution)/shard_map/dot_general | solution.py:70
  401.8 5.2 %all-reduce.13.cloned.1.call-done = bf16[192,1024]{1,0:T(8,128)(2,1)} async-done(((bf16[192,1024]{1,0:T(8,128)(2,1)}), bf16[192,1024]{1,0:T(8,128)(2,1)}) %all-reduce.13.cloned.1.call-update) | async-done | bytes 393232 | tf_op jit(solution)/shard_map/psum | solution.py:78
  407.0 2.2 fusion.34
  409.2 0.0 copy-done.2
  409.2 6.7 %fusion.35 = f32[1792,1024]{1,0:T(8,128)} fusion(bf16[192,1792]{1,0:T(8,128)(2,1)S(1)} %copy-done.2, bf16[192,1024]{1,0:T(8,128)(2,1)} %all-reduce.13.cloned.1.call-done, f32[192,1024]{1,0:T(8,128)} %all-reduce.7.cloned.1.call-done, f32[1024]{0:T(1024)S(1)} %copy-done.6), kind=kOutput, calls=%fused_computation.44 | convolution fusion | flops 4229431296 | bytes 9211904 | tf_op jit(solution)/shard_map/dot_general | solution.py:81
  (6 shorter events, 0.0 us)
Async XLA Ops:
  7.2 70.5 %copy-start = (bf16[896,1792]{1,0:T(8,128)(2,1)S(1)}, bf16[896,1792]{1,0:T(8,128)(2,1)}, u32[]{:S(2)}) copy-start(bf16[896,1792]{1,0:T(8,128)(2,1)} %param.14) | copy-start | bytes 9633796
  7.2 67.2 %reduce-scatter.4.cloned.1.call-start = ((), (), s32[]{:S(2)}) async-start(), calls=%async_computation.1 | async-start | bytes 2064384 | tf_op jit(solution)/shard_map/reduce_scatter | solution.py:46
  69.6 160.9 %all-reduce.7.cloned.1.call-start = ((), (), s32[]{:S(2)}) async-start(), calls=%async_computation.2 | async-start | bytes 1572864 | tf_op jit(solution)/shard_map/psum | solution.py:62
  77.7 65.9 %copy-start.9 = (u32[32]{0:T(128)S(1)}, u32[32]{0:T(128)}, u32[]{:S(2)}) copy-start(u32[32]{0:T(128)} %constant.30) | copy-start | bytes 388
  79.6 77.5 %copy-start.4 = (bf16[12,1792]{1,0:T(8,128)(2,1)S(1)}, bf16[12,1792]{1,0:T(8,128)(2,1)}, u32[]{:S(2)}) copy-start(bf16[12,1792]{1,0:T(8,128)(2,1)} %param.10) | copy-start | bytes 129028
  79.6 77.5 %copy-start.8 = (f32[1792]{0:T(1024)S(1)}, f32[1792]{0:T(1024)}, u32[]{:S(2)}) copy-start(f32[1792]{0:T(1024)} %param.15) | copy-start | bytes 21508
  132.6 13.1 %collective-permute-start.2 = (f32[16,1792]{1,0:T(8,128)S(1)}, f32[16,1792]{1,0:T(8,128)S(1)}, u32[]{:S(2)}, u32[]{:S(2)}) collective-permute-start(f32[16,1792]{1,0:T(8,128)S(1)} %fusion), channel_id=1, source_target_pairs={{0,3},{1,4},{2,5},{3,6},{4,7},{5,8},{6,9},{7,10},{8,11},{9,12},{10... | collective-permute-start | bytes 344072
  133.9 11.8 %collective-permute-start.1 = (f32[16,1792]{1,0:T(8,128)S(1)}, f32[16,1792]{1,0:T(8,128)}, u32[]{:S(2)}, u32[]{:S(2)}) collective-permute-start(f32[16,1792]{1,0:T(8,128)S(1)} %fusion), channel_id=1, source_target_pairs={{0,2},{1,3},{2,4},{3,5},{4,6},{5,7},{6,8},{7,9},{8,10},{9,11},{10,... | collective-permute-start | bytes 344072
  138.4 7.3 %collective-permute-start = (f32[16,1792]{1,0:T(8,128)S(1)}, f32[16,1792]{1,0:T(8,128)}, u32[]{:S(2)}, u32[]{:S(2)}) collective-permute-start(f32[16,1792]{1,0:T(8,128)S(1)} %fusion), channel_id=1, source_target_pairs={{0,1},{1,2},{2,3},{3,4},{4,5},{5,6},{6,7},{7,8},{8,9},{9,10},{10,1... | collective-permute-start | bytes 344072
  141.2 4.4 %collective-permute-start.3 = (f32[12,1792]{1,0:T(8,128)}, f32[12,1792]{1,0:T(8,128)}, u32[]{:S(2)}, u32[]{:S(2)}) collective-permute-start(f32[12,1792]{1,0:T(8,128)} %slice.10), channel_id=1, source_target_pairs={{0,4},{1,5},{2,6},{3,7},{4,8},{5,9},{6,10},{7,11},{8,12},{9,13},{1... | collective-permute-start | bytes 258056
  158.1 57.1 %copy-start.5 = (bf16[12,1792]{1,0:T(8,128)(2,1)}, bf16[12,1792]{1,0:T(8,128)(2,1)S(1)}, u32[]{:S(2)}) copy-start(bf16[12,1792]{1,0:T(8,128)(2,1)S(1)} %fusion.23) | copy-start | bytes 129028
  207.9 22.6 %copy-start.6 = (f32[1024]{0:T(1024)S(1)}, f32[1024]{0:T(1024)}, u32[]{:S(2)}) copy-start(f32[1024]{0:T(1024)} %param.17) | copy-start | bytes 12292
  215.3 73.7 %all-reduce.9.cloned.1.call-start = ((), (), s32[]{:S(2)}) async-start(), calls=%async_computation.3 | async-start | bytes 2752512 | tf_op jit(solution)/shard_map/psum | solution.py:67
  240.4 136.8 %copy-start.7 = (f32[1792]{0:T(1024)S(1)}, f32[1792]{0:T(1024)}, u32[]{:S(2)}) copy-start(f32[1792]{0:T(1024)} %param.19) | copy-start | bytes 21508
  240.4 136.8 %all-reduce.11.cloned.1.call-start = ((), (), s32[]{:S(2)}) async-start(), calls=%async_computation.4 | async-start | bytes 2752512 | tf_op jit(solution)/shard_map/psum | solution.py:68
  288.9 118.1 %all-reduce.13.cloned.1.call-start = ((), (), s32[]{:S(2)}) async-start(), calls=%async_computation.5 | async-start | bytes 786432 | tf_op jit(solution)/shard_map/psum | solution.py:78
  389.1 2.5 copy-start.1
  389.2 2.5 copy-start.3
  407.0 2.2 copy-start.2
Sparse Core Ops, SparseCore 0:
  69.7 4.6 reduce-scatter.3
  215.4 15.0 all-reduce.6
  240.5 48.3 all-reduce.8
  292.7 84.3 all-reduce.10
  389.3 17.6 all-reduce.12
